TPU v7x, 256 devices: a whole 4x4x8 slice. The times are simulated.
256 devices in a mesh: hst: 16 (over z_lo, x), dev: 16 (over y, z_hi, core).
Axes of the slice: x: 4, y: 4, z: 8 (z_hi: 2, z_lo: 4; z = z_hi * 4 + z_lo), core: 2. Of those that a mesh axis runs over, the one named last changes fastest.
Arguments:
- grad_out: bfloat16 [32768, 6144], P(('hst', 'dev')), may hold values from -6 to 6
- gates: float32 [32768], P(('hst', 'dev')), may hold values from 0.1 to 1
- route_rows: int32 [8704], P(('hst', 'dev')), may hold values from 0 to 128, as said below
- saved_act: bfloat16 [8704, 8192], P(('hst', 'dev')), may hold values from -6 to 6
- queries: bfloat16 [32768, 768], P(('hst', 'dev')), may hold values from -64 to 64
- keys: bfloat16 [32768, 128], P(('hst', 'dev')), may hold values from -16 to 16
- values: bfloat16 [32768, 128], P(('hst', 'dev')), may hold values from -6 to 6
- out_proj: bfloat16 [768, 6144], P(None, 'dev'), may hold values from -0.21875 to 0.21875
- w_down: bfloat16 [6144, 8192], P(None, 'dev'), may hold values from -0.0625 to 0.0625
Outputs:
- act_grad: bfloat16 [8704, 8192], P(('hst', 'dev'))
- query_grad: bfloat16 [32768, 768], P(('hst', 'dev'))
- key_grad: bfloat16 [32768, 128], P(('hst', 'dev'))
- value_grad: bfloat16 [32768, 128], P(('hst', 'dev'))
- proj_grad: float32 [768, 6144], P('hst', 'dev')
- down_grad: float32 [6144, 8192], P('hst', 'dev')
Inputs may be any that keep to these rules, and one draw needn't show every extreme that they name: `route_rows`: each block's 34 entries list distinct rows below 128 in increasing order, then 128 for the empty slots. At least half of every block's slots are used, and in some sequence every block uses all 34.
All inputs are finite; a program needn't handle non-finite values.
Results may differ from a plain program's by a relative error of at most 0.024.
Values may be sent and summed in bfloat16 or wider, within the bound.
No kernel may reach another device: no remote copies, remote signals or barrier semaphores. Data moves between devices by JAX's collectives and lax.ppermute only.
A program may use at most 128 MiB of HBM per device.

v0:
```python
import jax
import jax.numpy as jnp
from jax import lax
from jax.experimental import pallas as pl
from jax.experimental.pallas import tpu as pltpu
from jax.sharding import Mesh, PartitionSpec as P

HEAD = 128
SLOT_PAD = 40
F32 = jnp.float32
BF16 = jnp.bfloat16


def shift(value, axis, by):
    size = lax.axis_size(axis)
    return lax.ppermute(value, axis, [(i, (i + by) % size) for i in range(size)])


def add32(*terms):
    total = terms[0].astype(F32)
    for term in terms[1:]:
        total = total + term.astype(F32)
    return total


CHIPS = ("y", "core")
GROUP = ("y", "zh", "core")
SEQUENCES = ("zl", "x")


def swap(value, axes):
    return lax.all_to_all(value, axes, 0, 0, tiled=True)


def meet(*values):
    return lax.optimization_barrier(values)


def ring_pieces(value):
    return [value, shift(value, "y", -1), shift(value, "y", 2), shift(value, "y", 1)]


def pick(array, index):
    return lax.dynamic_index_in_dim(array, index, 0, keepdims=False)


def join_rows(joined, pieces):
    start = 0
    for piece in pieces:
        joined[start : start + piece.shape[0], :] = piece[...]
        start += piece.shape[0]


def down_product(spots, pieces, act_all):
    count, rows, hidden = act_all.shape
    width = pieces[0].shape[1]
    tile = width // 8
    piece_rows = pieces[0].shape[0]

    def kernel(spots_ref, near_ref, far_ref, act_ref, out_ref, joined, acts):
        @pl.when(pl.program_id(0) == 0)
        def _():
            for i in range(count):
                acts[rows * i : rows * (i + 1), :] = act_ref[spots_ref[i]]

        join_rows(joined, (near_ref, far_ref))
        out_ref[...] = lax.dot_general(
            joined[...], acts[...], (((0,), (0,)), ((), ())), preferred_element_type=F32
        ).astype(BF16)

    return pl.pallas_call(
        kernel,
        grid_spec=pltpu.PrefetchScalarGridSpec(
            num_scalar_prefetch=1,
            grid=(8,),
            in_specs=[pl.BlockSpec((piece_rows, tile), lambda i, s: (0, i))] * 2
            + [pl.BlockSpec((count, rows, hidden), lambda i, s: (0, 0, 0))],
            out_specs=pl.BlockSpec((tile, hidden), lambda i, s: (i, 0)),
            scratch_shapes=[pltpu.VMEM((count * rows, tile), BF16), pltpu.VMEM((count * rows, hidden), BF16)],
        ),
        out_shape=jax.ShapeDtypeStruct((width, hidden), BF16),
        compiler_params=pltpu.CompilerParams(vmem_limit_bytes=60 * 2**20),
        cost_estimate=pl.CostEstimate(
            flops=2 * count * rows * width * hidden, bytes_accessed=16 * 2**20, transcendentals=0
        ),
    )(spots, *pieces, act_all)


def act_product(spots, pieces, w_down):
    rows, held = SLOT_PAD, len(pieces)
    count = sum(p.shape[0] for p in pieces) // rows
    width, hidden = w_down.shape
    steps = 4
    tile = width // steps

    def kernel(spots_ref, *refs):
        w_ref, out_ref, joined, total = refs[held:]
        step = pl.program_id(0)
        join_rows(joined, refs[:held])
        term = jnp.dot(joined[...], w_ref[...], preferred_element_type=F32)

        @pl.when(step == 0)
        def _():
            total[...] = term

        @pl.when(step > 0)
        def _():
            total[...] += term

        @pl.when(step == steps - 1)
        def _():
            for i in range(count):
                out_ref[spots_ref[i]] = total[rows * i : rows * (i + 1), :].astype(BF16)

    return pl.pallas_call(
        kernel,
        grid_spec=pltpu.PrefetchScalarGridSpec(
            num_scalar_prefetch=1,
            grid=(steps,),
            in_specs=[pl.BlockSpec((p.shape[0], tile), lambda i, s: (0, i)) for p in pieces]
            + [pl.BlockSpec((tile, hidden), lambda i, s: (i, 0))],
            out_specs=pl.BlockSpec((count, rows, hidden), lambda i, s: (0, 0, 0)),
            scratch_shapes=[pltpu.VMEM((count * rows, tile), BF16), pltpu.VMEM((count * rows, hidden), F32)],
        ),
        out_shape=jax.ShapeDtypeStruct((count, rows, hidden), BF16),
        compiler_params=pltpu.CompilerParams(vmem_limit_bytes=60 * 2**20),
        cost_estimate=pl.CostEstimate(
            flops=2 * count * rows * width * hidden, bytes_accessed=16 * 2**20, transcendentals=0
        ),
    )(spots, *pieces, w_down)


def over_zl(mine):
    zl = lax.axis_index("zl")
    return add32(pick(mine, zl), *[shift(pick(mine, (zl + e) % 4), "zl", e) for e in (1, 2, 3)])


def attn_product(where, cols_all, out_proj, other_proj):
    _, tokens, both = cols_all.shape
    features, cols = out_proj.shape

    def kernel(where_ref, *refs):
        col_refs, own_ref, other_ref, mine_ref, theirs_ref, joined = refs[:4], *refs[4:]
        for d in range(4):
            joined[tokens * d : tokens * (d + 1), :] = col_refs[d][0]
        near = pl.multiple_of(where_ref[2] * cols, 128)
        far = pl.multiple_of((1 - where_ref[2]) * cols, 128)
        by_cols = (((1,), (1,)), ((), ()))
        product = lax.dot_general(
            joined[:, pl.ds(near, cols)], own_ref[...], by_cols, preferred_element_type=F32
        ) + lax.dot_general(joined[:, pl.ds(far, cols)], other_ref[...], by_cols, preferred_element_type=F32)
        product = product.astype(BF16).reshape(4, tokens, features)

        @pl.when(pl.program_id(0) == 0)
        def _():
            theirs_ref[...] = product

        @pl.when(pl.program_id(0) == 1)
        def _():
            mine_ref[...] = product

    def spot(d):
        return lambda i, s: (((s[0] + d) % 4) * 2 + (s[1] + 1 - i) % 2, 0, 0)

    whole = pl.BlockSpec((features, cols), lambda i, s: (0, 0))
    out = pl.BlockSpec((4, tokens, features), lambda i, s: (0, 0, 0))
    return pl.pallas_call(
        kernel,
        grid_spec=pltpu.PrefetchScalarGridSpec(
            num_scalar_prefetch=1,
            grid=(2,),
            in_specs=[pl.BlockSpec((1, tokens, both), spot(d)) for d in range(4)] + [whole, whole],
            out_specs=[out, out],
            scratch_shapes=[pltpu.VMEM((4 * tokens, both), BF16)],
        ),
        out_shape=[jax.ShapeDtypeStruct((4, tokens, features), BF16)] * 2,
        compiler_params=pltpu.CompilerParams(vmem_limit_bytes=48 * 2**20),
        cost_estimate=pl.CostEstimate(
            flops=16 * tokens * both * features, bytes_accessed=6 * 2**20, transcendentals=0
        ),
    )(where, *[cols_all] * 4, out_proj, other_proj)


def proj_product(where, mine, partner, cols_all):
    _, tokens, features = mine.shape
    both = cols_all.shape[2]

    rows = features // 16

    def kernel(where_ref, mine_ref, partner_ref, cols_ref, *refs):
        outs, (joined, sides, product) = refs[:4], refs[4:]
        for d in range(4):
            row = lax.rem(where_ref[0] + d, 4) * 2
            for f, ref in ((0, mine_ref), (1, partner_ref)):
                start = tokens * (2 * d + f)
                joined[start : start + tokens, :] = ref[d]
                sides[start : start + tokens, :] = cols_ref[row + lax.rem(where_ref[1] + f, 2)]
        product[...] = lax.dot_general(
            joined[...], sides[...], (((0,), (0,)), ((), ())), preferred_element_type=F32
        )
        for d in range(4):
            column = lax.rem(where_ref[3] + d, 4)
            for z in range(4):
                start = pl.multiple_of((4 * z + column) * rows, 16)
                outs[d][z] = product[pl.ds(start, rows), :].astype(BF16)

    piece = pl.BlockSpec((4, rows, both), lambda i, s: (0, 0, 0))
    whole = pl.BlockSpec((4, tokens, features), lambda i, s: (0, 0, 0))
    return pl.pallas_call(
        kernel,
        grid_spec=pltpu.PrefetchScalarGridSpec(
            num_scalar_prefetch=1,
            grid=(1,),
            in_specs=[whole, whole, pl.BlockSpec((8, tokens, both), lambda i, s: (0, 0, 0))],
            out_specs=[piece] * 4,
            scratch_shapes=[
                pltpu.VMEM((8 * tokens, features), BF16),
                pltpu.VMEM((8 * tokens, both), BF16),
                pltpu.VMEM((features, both), F32),
            ],
        ),
        out_shape=[jax.ShapeDtypeStruct((4, rows, both), BF16)] * 4,
        compiler_params=pltpu.CompilerParams(vmem_limit_bytes=48 * 2**20),
        cost_estimate=pl.CostEstimate(
            flops=16 * tokens * both * features, bytes_accessed=6 * 2**20, transcendentals=0
        ),
    )(where, mine, partner, cols_all)


def on_device(grad_out, gates, route_rows, saved_act, queries, keys, values, out_proj, w_down):
    y, zh, core = lax.axis_index("y"), lax.axis_index("zh"), lax.axis_index("core")
    tokens, width = grad_out.shape
    slots = route_rows.shape[0]
    heads = queries.shape[1] // HEAD
    cols = out_proj.shape[1]
    hidden = w_down.shape[1]
    scale = HEAD ** (-0.5)

    kv = jnp.concatenate([keys, values], 1)
    kv_other = shift(kv, "zh", 1)

    rows = jnp.concatenate([route_rows, jnp.full((SLOT_PAD - slots,), tokens, jnp.int32)])
    hot = rows[:, None] == jnp.arange(tokens, dtype=jnp.int32)[None, :]
    picked = jnp.dot(hot.astype(BF16), grad_out, preferred_element_type=F32)
    gate = jnp.sum(jnp.where(hot, gates[None, :], 0.0), axis=1)
    upstream = (gate[:, None] * picked).astype(BF16)

    kv2 = jnp.stack([kv, kv_other])
    kv8 = jnp.stack(ring_pieces(kv2))
    all_kv = jnp.stack([kv8, shift(kv8, "core", 1)]).reshape(16 * tokens, 2 * HEAD)
    all_keys, all_values = all_kv[:, :HEAD], all_kv[:, HEAD:]

    near = lax.all_gather(upstream, CHIPS, axis=0, tiled=True)
    upstream, kv_other = meet(upstream, kv_other)
    other_up = shift(upstream, "zh", 1)

    act_in = jnp.concatenate([saved_act, jnp.zeros((SLOT_PAD - slots, saved_act.shape[1]), BF16)], 0)
    act_in = act_in.reshape(SLOT_PAD, 16, hidden).transpose(1, 0, 2)
    cols_in = grad_out.reshape(tokens, 4, 2, 2, cols).transpose(1, 3, 0, 2, 4).reshape(8, tokens, 2 * cols)
    other_up, out_proj, act_in, cols_in = meet(other_up, out_proj, act_in, cols_in)
    far = lax.all_gather(other_up, CHIPS, axis=0, tiled=True)
    pieces = (near, far)
    spots = jnp.stack(
        [py * 4 + (zh ^ e) * 2 + pc for e in range(2) for py in range(4) for pc in range(2)]
    ).astype(jnp.int32)

    kv2 = jnp.stack([kv, kv_other])
    kv8 = jnp.stack(ring_pieces(kv2))
    all_kv = jnp.stack([kv8, shift(kv8, "core", 1)]).reshape(16 * tokens, 2 * HEAD)
    all_keys, all_values = all_kv[:, :HEAD], all_kv[:, HEAD:]

    place = jnp.arange(16, dtype=jnp.int32)
    block = ((y + (place // 2) % 4) % 4) * 4 + (zh ^ (place % 2)) * 2 + (core ^ (place // 8))
    key_place = (block[:, None] * tokens + jnp.arange(tokens, dtype=jnp.int32)[None, :]).reshape(-1)
    query_place = (y * 4 + zh * 2 + core) * tokens + jnp.arange(tokens, dtype=jnp.int32)

    query3 = queries.reshape(tokens, heads, HEAD)
    scores = jnp.einsum("qhd,kd->hqk", query3, all_keys, preferred_element_type=F32) * scale
    allowed = key_place[None, :] <= query_place[:, None]
    scores = jnp.where(allowed[None], scores, jnp.float32(-1e30))
    highest = jnp.max(scores, axis=2, keepdims=True)
    weights = jnp.exp(scores - highest)
    probs = weights / jnp.sum(weights, axis=2, keepdims=True)
    probs_b = probs.astype(BF16)
    attended = jnp.einsum("hqk,kd->qhd", probs_b, all_values, preferred_element_type=F32).astype(BF16)

    flat = attended.reshape(tokens, heads * HEAD)
    other_proj = shift(out_proj, "zh", 1)
    spots, flat, other_proj = meet(spots, flat, other_proj)
    act_all = swap(act_in, GROUP)

    where = jnp.stack([y, core, zh, lax.axis_index("x")]).astype(jnp.int32)
    down = down_product(spots, pieces, act_all)

    cols_in, spots, where, down = meet(cols_in, spots, where, down)
    down_grad = lax.psum_scatter(down, SEQUENCES, scatter_dimension=0, tiled=True).astype(F32)
    cols_all = swap(cols_in, CHIPS)

    part = act_product(spots, pieces, w_down)

    att4 = jnp.stack(ring_pieces(flat))
    att_other = shift(att4, "core", 1)
    where, part = meet(where, part)
    mine, theirs = attn_product(where, cols_all, out_proj, other_proj)
    act_back = swap(part, GROUP)
    chip_sum = add32(mine, shift(theirs, "core", 1)).astype(BF16)
    attn_grad = add32(chip_sum[0], *[shift(chip_sum[d], "y", d) for d in (1, 2, 3)]).astype(BF16)

    where, attn_grad = meet(where, attn_grad)
    proj = proj_product(where, att4, att_other, cols_all)

    attn_grad3 = attn_grad.reshape(tokens, heads, HEAD)
    prob_grad = jnp.einsum("qhd,kd->hqk", attn_grad3, all_values, preferred_element_type=F32)
    row_dot = jnp.sum(attn_grad3.astype(F32) * attended.astype(F32), axis=2)
    score_grad = (probs * (prob_grad - row_dot.T[:, :, None])).astype(BF16)
    query_grad = jnp.einsum("hqk,kd->qhd", score_grad, all_keys, preferred_element_type=F32) * scale
    query_grad = query_grad.astype(BF16).reshape(tokens, heads * HEAD)
    key_part = jnp.einsum("hqk,qhd->kd", score_grad, query3, preferred_element_type=F32) * scale
    value_part = jnp.einsum("hqk,qhd->kd", probs_b, attn_grad3, preferred_element_type=F32)
    kv_part = jnp.concatenate([key_part, value_part], axis=1).astype(BF16)
    kv_part = kv_part.reshape(2, 4, 2, tokens, 2 * HEAD)
    kv_chip = add32(kv_part[0], shift(kv_part[1], "core", 1)).astype(BF16)
    kv_ring = add32(kv_chip[0], *[shift(kv_chip[d], "y", d) for d in (1, 2, 3)]).astype(BF16)
    proj = add32(proj[0], *[shift(proj[d], "x", d) for d in (1, 2, 3)]).astype(BF16)
    act_back, proj, kv_ring = meet(act_back, proj, kv_ring)
    act_grad = act_back.transpose(1, 0, 2).reshape(SLOT_PAD, 16 * hidden)[:slots]
    proj = over_zl(proj)
    left, right = proj[:, :cols], proj[:, cols:]
    keep = jnp.where(zh == 0, left, right)
    give = jnp.where(zh == 0, right, left).astype(BF16)
    proj_grad = keep + shift(give, "zh", 1).astype(F32)

    kv_grad = add32(kv_ring[0], shift(kv_ring[1], "zh", 1)).astype(BF16)
    return act_grad, query_grad, kv_grad[:, :HEAD], kv_grad[:, HEAD:], proj_grad, down_grad


def solution(mesh):
    axes = ("zl", "x", "y", "zh", "core")
    fine = Mesh(mesh.devices.reshape(4, 4, 4, 2, 2), axes)
    by_token = P(axes, None)
    by_dev = P(None, ("y", "zh", "core"))
    both = P(("zl", "x"), ("y", "zh", "core"))
    return jax.shard_map(
        on_device,
        mesh=fine,
        in_specs=(by_token, P(axes), P(axes), by_token, by_token, by_token, by_token, by_dev, by_dev),
        out_specs=(by_token, by_token, by_token, by_token, both, both),
        check_vma=False,
    )
```

profile of v0, /device:TPU:6, one launch (start us, length us, event | category | flops | bytes accessed | tf_op | source)
XLA Modules:
  0.0 261.2 jit_solution(18111138442802704051)
XLA Ops:
  13.0 7.3 %collective-permute-start = (bf16[128,256]{1,0:T(8,128)(2,1)S(1)}, bf16[128,256]{1,0:T(8,128)(2,1)S(1)}, u32[]{:S(2)}, u32[]{:S(2)}) collective-permute-start(bf16[128,256]{1,0:T(8,128)(2,1)S(1)} %constant_dynamic-update-slice_fusion), channel_id=1, source_target_pairs={{0,2},{2,0},{1,3},{3,1},{4,6},{6,4},{5,7},{7,5},{8,10},{10,8},{9,1... | collective-permute-start | bytes 196616 | tf_op jit(solution)/shard_map/ppermute | solution.py:16
  22.7 6.4 %collective-permute-start.1 = (bf16[40,6144]{1,0:T(8,128)(2,1)}, bf16[40,6144]{1,0:T(8,128)(2,1)}, u32[]{:S(2)}, u32[]{:S(2)}) collective-permute-start(bf16[40,6144]{1,0:T(8,128)(2,1)} %fusion.1), channel_id=1, source_target_pairs={{0,2},{2,0},{1,3},{3,1},{4,6},{6,4},{5,7},{7,5},{8,10},{10,8},{9,1... | collective-permute-start | bytes 1474568 | tf_op jit(solution)/shard_map/ppermute | solution.py:16
  35.5 5.9 %collective-permute-done.1 = bf16[40,6144]{1,0:T(8,128)(2,1)} collective-permute-done((bf16[40,6144]{1,0:T(8,128)(2,1)}, bf16[40,6144]{1,0:T(8,128)(2,1)}, u32[]{:S(2)}, u32[]{:S(2)}) %collective-permute-start.1) | collective-permute-done | bytes 491552 | tf_op jit(solution)/shard_map/ppermute | solution.py:16
  53.6 11.7 %collective-permute-start.6 = (bf16[768,384]{1,0:T(8,128)(2,1)S(1)}, bf16[768,384]{1,0:T(8,128)(2,1)S(1)}, u32[]{:S(2)}, u32[]{:S(2)}) collective-permute-start(bf16[768,384]{1,0:T(8,128)(2,1)S(1)} %copy-done), channel_id=1, source_target_pairs={{0,2},{2,0},{1,3},{3,1},{4,6},{6,4},{5,7},{7,5},{8,10},{10,8},{9,1... | collective-permute-start | bytes 1769480 | tf_op jit(solution)/shard_map/ppermute | solution.py:16
  65.4 3.9 %all-to-all-start = ((bf16[16,40,512]{2,1,0:T(8,128)(2,1)}), bf16[16,40,512]{2,1,0:T(8,128)(2,1)S(1)}, u32[]{:S(2)}, u32[]{:S(2)}) async-start(bf16[16,40,512]{2,1,0:T(8,128)(2,1)} %bitcast.154), calls=%async_computation | async-start | bytes 1310720 | tf_op jit(solution)/shard_map/all_to_all | solution.py:32
  71.5 6.2 %fusion.43 = (f32[6,128]{1,0:T(8,128)S(1)}, f32[6,128,2048]{1,2,0:T(8,128)}) fusion(pred[128,2048]{0,1:T(8,128)(4,1)} %broadcast_compare_fusion, bf16[128,6,128]{0,2,1:T(8,128)(2,1)} %bitcast.176, bf16[2048,256]{1,0:T(8,128)(2,1)S(1)} %bitcast.158), kind=kOutput, calls=%fused_computation.106 | convolution fusion | flops 408946688 | bytes 7277568 | tf_op jit(solution)/shard_map/sub | solution.py:282
  77.7 3.4 %fusion.8 = bf16[6,128,2048]{1,2,0:T(8,128)(2,1)S(1)} fusion(f32[6,128,2048]{1,2,0:T(8,128)} %get-tuple-element.94, f32[6,128]{1,0:T(8,128)S(1)} %get-tuple-element.93), kind=kLoop, calls=%fused_computation.13 | loop fusion | flops 3145728 | bytes 9440256 | tf_op jit(solution)/shard_map/convert_element_type | solution.py:284
  82.9 22.5 %all-to-all-done.act_ref = bf16[16,40,512]{2,1,0:T(8,128)(2,1)S(1)} async-done(((bf16[16,40,512]{2,1,0:T(8,128)(2,1)}), bf16[16,40,512]{2,1,0:T(8,128)(2,1)S(1)}, u32[]{:S(2)}, u32[]{:S(2)}) %all-to-all-start) | async-done | bytes 655392 | tf_op jit(solution)/shard_map/all_to_all | solution.py:32
  106.3 11.7 %shard_map.136 = bf16[6144,512]{1,0:T(8,128)(2,1)} custom-call(s32[16]{0:T(128)} %stack.130.spots_ref, bf16[320,6144]{1,0:T(8,128)(2,1)} %all-gather.3.cloned.1.call-done.near_ref.refs_0_, bf16[320,6144]{1,0:T(8,128)(2,1)} %all-gather.5.cloned.1.call-done.far_ref.refs_1_, bf16[16,40,512]{2,1,0:T(8,128)(2,1)} %copy-done.6), custom_call_target="tpu_custom_call" | custom-call | flops 4026531840 | bytes 16777216 | tf_op jit(solution)/shard_map/pallas_call | solution.py:71
  118.0 3.9 %all-to-all-start.2 = ((bf16[8,128,768]{2,1,0:T(8,128)(2,1)}), bf16[8,128,768]{2,1,0:T(8,128)(2,1)S(1)}, u32[]{:S(2)}, u32[]{:S(2)}) async-start(bf16[8,128,768]{2,1,0:T(8,128)(2,1)} %reshape.165), calls=%async_computation.2 | async-start | bytes 3145728 | tf_op jit(solution)/shard_map/all_to_all | solution.py:32
  121.9 9.6 %shard_map.137 = bf16[16,40,512]{2,1,0:T(8,128)(2,1)} custom-call(s32[16]{0:T(128)} %stack.130.spots_ref, bf16[320,6144]{1,0:T(8,128)(2,1)} %all-gather.3.cloned.1.call-done.near_ref.refs_0_, bf16[320,6144]{1,0:T(8,128)(2,1)} %all-gather.5.cloned.1.call-done.far_ref.refs_1_, bf16[6144,512]{1,0:T(8,128)(2,1)} %refs_2_.1), custom_call_target="tpu_custom_call" | custom-call | flops 4026531840 | bytes 16777216 | tf_op jit(solution)/shard_map/pallas_call | solution.py:115
  131.5 12.0 %all-to-all-done.2.refs_0_.refs_1_.refs_2_.refs_3_.cols_ref = bf16[8,128,768]{2,1,0:T(8,128)(2,1)S(1)} async-done(((bf16[8,128,768]{2,1,0:T(8,128)(2,1)}), bf16[8,128,768]{2,1,0:T(8,128)(2,1)S(1)}, u32[]{:S(2)}, u32[]{:S(2)}) %all-to-all-start.2) | async-done | bytes 1572896 | tf_op jit(solution)/shard_map/all_to_all | solution.py:32
  143.4 3.6 %shard_map.138 = (bf16[4,128,768]{2,1,0:T(8,128)(2,1)S(1)}, bf16[4,128,768]{2,1,0:T(8,128)(2,1)}) custom-call(s32[4]{0:T(128)S(1)} %pad_add_fusion.where_ref, bf16[8,128,768]{2,1,0:T(8,128)(2,1)S(1)} %all-to-all-done.2.refs_0_.refs_1_.refs_2_.refs_3_.cols_ref, bf16[8,128,768]{2,1,0:T(8,128)(2,1)S(1)} %all-to-all-done.2.refs_0_.refs_1_.refs_2_.refs_3_.cols_ref, ...), custom_call_target="tpu_custom_call" | custom-call | flops 1207959552 | bytes 6291456 | tf_op jit(solution)/shard_map/pallas_call | solution.py:167
  155.3 9.9 %collective-permute-done.13 = bf16[128,768]{1,0:T(8,128)(2,1)S(1)} collective-permute-done((bf16[128,768]{1,0:T(8,128)(2,1)S(1)}, bf16[128,768]{1,0:T(8,128)(2,1)S(1)}, u32[]{:S(2)}, u32[]{:S(2)}) %collective-permute-start.13) | collective-permute-done | bytes 196640 | tf_op jit(solution)/shard_map/ppermute | solution.py:16
  166.5 6.3 %collective-permute-done.8 = bf16[128,768]{1,0:T(8,128)(2,1)S(1)} collective-permute-done((bf16[128,768]{1,0:T(8,128)(2,1)S(1)}, bf16[128,768]{1,0:T(8,128)(2,1)S(1)}, u32[]{:S(2)}, u32[]{:S(2)}) %collective-permute-start.8) | collective-permute-done | bytes 196640 | tf_op jit(solution)/shard_map/ppermute | solution.py:16
  175.7 4.2 %fusion.3 = bf16[6,128,2048]{1,2,0:T(8,128)(2,1)S(1)} fusion(bf16[128,6,128]{0,2,1:T(8,128)(2,1)S(1)} %bitcast.165, f32[6,128]{1,0:T(8,128)S(1)} %bitcast.183, f32[6,128,2048]{1,2,0:T(8,128)} %get-tuple-element.94, f32[6,128]{1,0:T(8,128)S(1)} %get-tuple-element.93, bf16[2048,256]{1,0:T(8,128)(2,1)} %bitcast.160), kind=kOutput, calls=%fused_computation.5 | convolution fusion | flops 408944640 | bytes 10164224 | tf_op jit(solution)/shard_map/qhd,kd->hqk/dot_general | solution.py:313
  185.6 7.7 %all-to-all-start.1 = ((bf16[16,40,512]{2,1,0:T(8,128)(2,1)}), bf16[16,40,512]{2,1,0:T(8,128)(2,1)}, u32[]{:S(2)}, u32[]{:S(2)}) async-start(bf16[16,40,512]{2,1,0:T(8,128)(2,1)} %shard_map.137), calls=%async_computation.1 | async-start | bytes 1310720 | tf_op jit(solution)/shard_map/all_to_all | solution.py:32
  193.2 3.2 %shard_map.139 = (bf16[4,48,768]{2,1,0:T(8,128)(2,1)S(1)}, bf16[4,48,768]{2,1,0:T(8,128)(2,1)}, bf16[4,48,768]{2,1,0:T(8,128)(2,1)}, bf16[4,48,768]{2,1,0:T(8,128)(2,1)}) custom-call(s32[4]{0:T(128)S(1)} %pad_add_fusion.where_ref, bf16[4,128,768]{2,1,0:T(8,128)(2,1)S(1)} %pad_maximum_fusion.1.mine_ref, ...), custom_call_target="tpu_custom_call" | custom-call | flops 1207959552 | bytes 6291456 | tf_op jit(solution)/shard_map/pallas_call | solution.py:209
  206.8 3.2 %collective-permute-start.21 = (bf16[2,128,256]{2,1,0:T(8,128)(2,1)S(1)}, bf16[2,128,256]{2,1,0:T(8,128)(2,1)S(1)}, u32[]{:S(2)}, u32[]{:S(2)}) collective-permute-start(bf16[2,128,256]{2,1,0:T(8,128)(2,1)S(1)} %get-tuple-element.82), channel_id=1, source_target_pairs={{0,12},{4,0},{8,4},{12,8},{1,13},{5,1},{9,5},{13,9},{2,14},{6,2},{... | collective-permute-start | bytes 393224 | tf_op jit(solution)/shard_map/ppermute | solution.py:16
  212.0 8.9 %collective-permute-done.16 = bf16[4,48,768]{2,1,0:T(8,128)(2,1)S(1)} collective-permute-done((bf16[4,48,768]{2,1,0:T(8,128)(2,1)}, bf16[4,48,768]{2,1,0:T(8,128)(2,1)S(1)}, u32[]{:S(2)}, u32[]{:S(2)}) %collective-permute-start.16) | collective-permute-done | bytes 294944 | tf_op jit(solution)/shard_map/ppermute | solution.py:16
  225.7 4.2 %collective-permute-start.22 = (bf16[128,256]{1,0:T(8,128)(2,1)S(1)}, bf16[128,256]{1,0:T(8,128)(2,1)S(1)}, u32[]{:S(2)}, u32[]{:S(2)}) collective-permute-start(bf16[128,256]{1,0:T(8,128)(2,1)S(1)} %slice_bitcast_fusion.19), channel_id=1, source_target_pairs={{0,2},{2,0},{1,3},{3,1},{4,6},{6,4},{5,7},{7,5},{8,10},{10,8},{9,1... | collective-permute-start | bytes 196616 | tf_op jit(solution)/shard_map/ppermute | solution.py:16
  229.9 6.5 %collective-permute-start.25 = (bf16[48,768]{1,0:T(8,128)(2,1)S(1)}, bf16[48,768]{1,0:T(8,128)(2,1)S(1)}, u32[]{:S(2)}, u32[]{:S(2)}) collective-permute-start(bf16[48,768]{1,0:T(8,128)(2,1)S(1)} %get-tuple-element.87), channel_id=1, source_target_pairs={{0,192},{64,0},{128,64},{192,128},{1,193},{65,1},{129,65},{193,129... | collective-permute-start | bytes 221192 | tf_op jit(solution)/shard_map/ppermute | solution.py:16
  239.0 5.0 %collective-permute-done.24 = bf16[48,768]{1,0:T(8,128)(2,1)S(1)} collective-permute-done((bf16[48,768]{1,0:T(8,128)(2,1)S(1)}, bf16[48,768]{1,0:T(8,128)(2,1)S(1)}, u32[]{:S(2)}, u32[]{:S(2)}) %collective-permute-start.24) | collective-permute-done | bytes 73760 | tf_op jit(solution)/shard_map/ppermute | solution.py:16
  246.6 5.4 %collective-permute-done.26 = bf16[48,384]{1,0:T(8,128)(2,1)S(1)} collective-permute-done((bf16[48,384]{1,0:T(8,128)(2,1)S(1)}, bf16[48,384]{1,0:T(8,128)(2,1)S(1)}, u32[]{:S(2)}, u32[]{:S(2)}) %collective-permute-start.26) | collective-permute-done | bytes 36896 | tf_op jit(solution)/shard_map/ppermute | solution.py:16
  (122 shorter events, 74.5 us)
Async XLA Ops:
  7.2 98.3 %all-gather.3.cloned.1.call-start = ((), (), s32[]{:S(2)}) async-start(), calls=%async_computation.4 | async-start | bytes 4423680 | tf_op jit(solution)/shard_map/all_gather | solution.py:253
  11.4 94.0 %all-gather.5.cloned.1.call-start = ((), (), s32[]{:S(2)}) async-start(), calls=%async_computation.5 | async-start | bytes 4423680 | tf_op jit(solution)/shard_map/all_gather | solution.py:261
  13.0 9.7 %collective-permute-start = (bf16[128,256]{1,0:T(8,128)(2,1)S(1)}, bf16[128,256]{1,0:T(8,128)(2,1)S(1)}, u32[]{:S(2)}, u32[]{:S(2)}) collective-permute-start(bf16[128,256]{1,0:T(8,128)(2,1)S(1)} %constant_dynamic-update-slice_fusion), channel_id=1, source_target_pairs={{0,2},{2,0},{1,3},{3,1},{4,6},{6,4},{5,7},{7,5},{8,10},{10,8},{9,1... | collective-permute-start | bytes 196616 | tf_op jit(solution)/shard_map/ppermute | solution.py:16
  22.7 18.7 %collective-permute-start.1 = (bf16[40,6144]{1,0:T(8,128)(2,1)}, bf16[40,6144]{1,0:T(8,128)(2,1)}, u32[]{:S(2)}, u32[]{:S(2)}) collective-permute-start(bf16[40,6144]{1,0:T(8,128)(2,1)} %fusion.1), channel_id=1, source_target_pairs={{0,2},{2,0},{1,3},{3,1},{4,6},{6,4},{5,7},{7,5},{8,10},{10,8},{9,1... | collective-permute-start | bytes 1474568 | tf_op jit(solution)/shard_map/ppermute | solution.py:16
  52.4 17.1 %collective-permute-start.5 = (bf16[4,2,128,256]{3,2,1,0:T(8,128)(2,1)S(1)}, bf16[4,2,128,256]{3,2,1,0:T(8,128)(2,1)S(1)}, u32[]{:S(2)}, u32[]{:S(2)}) collective-permute-start(bf16[4,2,128,256]{3,2,1,0:T(8,128)(2,1)S(1)} %get-tuple-element.85), channel_id=1, source_target_pairs={{0,1},{1,0},{2,3},{3,2},{4,5},{5,4},{6,7},{7,6},{8,9},{9,8},{10,11... | collective-permute-start | bytes 1572872 | tf_op jit(solution)/shard_map/ppermute | solution.py:16
  53.6 29.2 %collective-permute-start.6 = (bf16[768,384]{1,0:T(8,128)(2,1)S(1)}, bf16[768,384]{1,0:T(8,128)(2,1)S(1)}, u32[]{:S(2)}, u32[]{:S(2)}) collective-permute-start(bf16[768,384]{1,0:T(8,128)(2,1)S(1)} %copy-done), channel_id=1, source_target_pairs={{0,2},{2,0},{1,3},{3,1},{4,6},{6,4},{5,7},{7,5},{8,10},{10,8},{9,1... | collective-permute-start | bytes 1769480 | tf_op jit(solution)/shard_map/ppermute | solution.py:16
  65.4 40.1 %all-to-all-start = ((bf16[16,40,512]{2,1,0:T(8,128)(2,1)}), bf16[16,40,512]{2,1,0:T(8,128)(2,1)S(1)}, u32[]{:S(2)}, u32[]{:S(2)}) async-start(bf16[16,40,512]{2,1,0:T(8,128)(2,1)} %bitcast.154), calls=%async_computation | async-start | bytes 1310720 | tf_op jit(solution)/shard_map/all_to_all | solution.py:32
  69.3 183.4 %reduce-scatter.2.cloned.1.call-start = ((), (), s32[]{:S(2)}) async-start(), calls=%async_computation.6 | async-start | bytes 6684672 | tf_op jit(solution)/shard_map/reduce_scatter | solution.py:296
  118.0 25.4 %all-to-all-start.2 = ((bf16[8,128,768]{2,1,0:T(8,128)(2,1)}), bf16[8,128,768]{2,1,0:T(8,128)(2,1)S(1)}, u32[]{:S(2)}, u32[]{:S(2)}) async-start(bf16[8,128,768]{2,1,0:T(8,128)(2,1)} %reshape.165), calls=%async_computation.2 | async-start | bytes 3145728 | tf_op jit(solution)/shard_map/all_to_all | solution.py:32
  148.2 17.0 %collective-permute-start.13 = (bf16[128,768]{1,0:T(8,128)(2,1)S(1)}, bf16[128,768]{1,0:T(8,128)(2,1)S(1)}, u32[]{:S(2)}, u32[]{:S(2)}) collective-permute-start(bf16[128,768]{1,0:T(8,128)(2,1)S(1)} %copy.57), channel_id=1, source_target_pairs={{0,4},{4,8},{8,12},{12,0},{1,5},{5,9},{9,13},{13,1},{2,6},{6,10},{... | collective-permute-start | bytes 589832 | tf_op jit(solution)/shard_map/ppermute | solution.py:16
  148.8 16.4 %collective-permute-start.12 = (bf16[128,768]{1,0:T(8,128)(2,1)S(1)}, bf16[128,768]{1,0:T(8,128)(2,1)S(1)}, u32[]{:S(2)}, u32[]{:S(2)}) collective-permute-start(bf16[128,768]{1,0:T(8,128)(2,1)S(1)} %copy.57), channel_id=1, source_target_pairs={{0,8},{4,12},{8,0},{12,4},{1,9},{5,13},{9,1},{13,5},{2,10},{6,14},... | collective-permute-start | bytes 589832 | tf_op jit(solution)/shard_map/ppermute | solution.py:16
  150.9 14.3 %collective-permute-start.11 = (bf16[128,768]{1,0:T(8,128)(2,1)S(1)}, bf16[128,768]{1,0:T(8,128)(2,1)S(1)}, u32[]{:S(2)}, u32[]{:S(2)}) collective-permute-start(bf16[128,768]{1,0:T(8,128)(2,1)S(1)} %copy.57), channel_id=1, source_target_pairs={{0,12},{4,0},{8,4},{12,8},{1,13},{5,1},{9,5},{13,9},{2,14},{6,2},{... | collective-permute-start | bytes 589832 | tf_op jit(solution)/shard_map/ppermute | solution.py:16
  151.8 14.7 %collective-permute-start.10 = (bf16[128,768]{1,0:T(8,128)(2,1)S(1)}, bf16[128,768]{1,0:T(8,128)(2,1)S(1)}, u32[]{:S(2)}, u32[]{:S(2)}) collective-permute-start(bf16[128,768]{1,0:T(8,128)(2,1)S(1)} %get-tuple-element.79), channel_id=1, source_target_pairs={{0,12},{4,0},{8,4},{12,8},{1,13},{5,1},{9,5},{13,9},{2,14},{6,2},{... | collective-permute-start | bytes 589832 | tf_op jit(solution)/shard_map/ppermute | solution.py:16
  153.2 13.3 %collective-permute-start.9 = (bf16[128,768]{1,0:T(8,128)(2,1)S(1)}, bf16[128,768]{1,0:T(8,128)(2,1)S(1)}, u32[]{:S(2)}, u32[]{:S(2)}) collective-permute-start(bf16[128,768]{1,0:T(8,128)(2,1)S(1)} %get-tuple-element.80), channel_id=1, source_target_pairs={{0,8},{4,12},{8,0},{12,4},{1,9},{5,13},{9,1},{13,5},{2,10},{6,14},... | collective-permute-start | bytes 589832 | tf_op jit(solution)/shard_map/ppermute | solution.py:16
  165.3 27.9 %collective-permute-start.14 = (bf16[4,128,768]{2,1,0:T(8,128)(2,1)S(1)}, bf16[4,128,768]{2,1,0:T(8,128)(2,1)S(1)}, u32[]{:S(2)}, u32[]{:S(2)}) collective-permute-start(bf16[4,128,768]{2,1,0:T(8,128)(2,1)S(1)} %pad_maximum_fusion.1.mine_ref), channel_id=1, source_target_pairs={{0,1},{1,0},{2,3},{3,2},{4,5},{5,4},{6,7},{7,6},{8,9},{9,8},{10,11... | collective-permute-start | bytes 2359304 | tf_op jit(solution)/shard_map/ppermute | solution.py:16
  185.6 20.0 %collective-permute-start.18 = (bf16[4,2,128,256]{3,2,1,0:T(8,128)(2,1)}, bf16[4,2,128,256]{3,2,1,0:T(8,128)(2,1)}, u32[]{:S(2)}, u32[]{:S(2)}) collective-permute-start(bf16[4,2,128,256]{3,2,1,0:T(8,128)(2,1)} %bitcast.171), channel_id=1, source_target_pairs={{0,1},{1,0},{2,3},{3,2},{4,5},{5,4},{6,7},{7,6},{8,9},{9,8},{10,11... | collective-permute-start | bytes 1572872 | tf_op jit(solution)/shard_map/ppermute | solution.py:16
  185.6 37.5 %all-to-all-start.1 = ((bf16[16,40,512]{2,1,0:T(8,128)(2,1)}), bf16[16,40,512]{2,1,0:T(8,128)(2,1)}, u32[]{:S(2)}, u32[]{:S(2)}) async-start(bf16[16,40,512]{2,1,0:T(8,128)(2,1)} %shard_map.137), calls=%async_computation.1 | async-start | bytes 1310720 | tf_op jit(solution)/shard_map/all_to_all | solution.py:32
  196.4 14.4 %collective-permute-start.17 = (bf16[4,48,768]{2,1,0:T(8,128)(2,1)}, bf16[4,48,768]{2,1,0:T(8,128)(2,1)S(1)}, u32[]{:S(2)}, u32[]{:S(2)}) collective-permute-start(bf16[4,48,768]{2,1,0:T(8,128)(2,1)} %get-tuple-element.52), channel_id=1, source_target_pairs={{0,48},{16,0},{32,16},{48,32},{1,49},{17,1},{33,17},{49,33},{2,50}... | collective-permute-start | bytes 884744 | tf_op jit(solution)/shard_map/ppermute | solution.py:16
  197.3 23.6 %collective-permute-start.16 = (bf16[4,48,768]{2,1,0:T(8,128)(2,1)}, bf16[4,48,768]{2,1,0:T(8,128)(2,1)S(1)}, u32[]{:S(2)}, u32[]{:S(2)}) collective-permute-start(bf16[4,48,768]{2,1,0:T(8,128)(2,1)} %get-tuple-element.51), channel_id=1, source_target_pairs={{0,32},{16,48},{32,0},{48,16},{1,33},{17,49},{33,1},{49,17},{2,34}... | collective-permute-start | bytes 884744 | tf_op jit(solution)/shard_map/ppermute | solution.py:16
  198.5 24.4 %collective-permute-start.15 = (bf16[4,48,768]{2,1,0:T(8,128)(2,1)}, bf16[4,48,768]{2,1,0:T(8,128)(2,1)S(1)}, u32[]{:S(2)}, u32[]{:S(2)}) collective-permute-start(bf16[4,48,768]{2,1,0:T(8,128)(2,1)} %get-tuple-element.50), channel_id=1, source_target_pairs={{0,16},{16,32},{32,48},{48,0},{1,17},{17,33},{33,49},{49,1},{2,18}... | collective-permute-start | bytes 884744 | tf_op jit(solution)/shard_map/ppermute | solution.py:16
  206.8 16.2 %collective-permute-start.21 = (bf16[2,128,256]{2,1,0:T(8,128)(2,1)S(1)}, bf16[2,128,256]{2,1,0:T(8,128)(2,1)S(1)}, u32[]{:S(2)}, u32[]{:S(2)}) collective-permute-start(bf16[2,128,256]{2,1,0:T(8,128)(2,1)S(1)} %get-tuple-element.82), channel_id=1, source_target_pairs={{0,12},{4,0},{8,4},{12,8},{1,13},{5,1},{9,5},{13,9},{2,14},{6,2},{... | collective-permute-start | bytes 393224 | tf_op jit(solution)/shard_map/ppermute | solution.py:16
  210.0 13.1 %collective-permute-start.20 = (bf16[2,128,256]{2,1,0:T(8,128)(2,1)S(1)}, bf16[2,128,256]{2,1,0:T(8,128)(2,1)S(1)}, u32[]{:S(2)}, u32[]{:S(2)}) collective-permute-start(bf16[2,128,256]{2,1,0:T(8,128)(2,1)S(1)} %get-tuple-element.83), channel_id=1, source_target_pairs={{0,8},{4,12},{8,0},{12,4},{1,9},{5,13},{9,1},{13,5},{2,10},{6,14},... | collective-permute-start | bytes 393224 | tf_op jit(solution)/shard_map/ppermute | solution.py:16
  210.8 12.2 %collective-permute-start.19 = (bf16[2,128,256]{2,1,0:T(8,128)(2,1)S(1)}, bf16[2,128,256]{2,1,0:T(8,128)(2,1)S(1)}, u32[]{:S(2)}, u32[]{:S(2)}) collective-permute-start(bf16[2,128,256]{2,1,0:T(8,128)(2,1)S(1)} %get-tuple-element.81), channel_id=1, source_target_pairs={{0,4},{4,8},{8,12},{12,0},{1,5},{5,9},{9,13},{13,1},{2,6},{6,10},{... | collective-permute-start | bytes 393224 | tf_op jit(solution)/shard_map/ppermute | solution.py:16
  225.7 11.7 %collective-permute-start.22 = (bf16[128,256]{1,0:T(8,128)(2,1)S(1)}, bf16[128,256]{1,0:T(8,128)(2,1)S(1)}, u32[]{:S(2)}, u32[]{:S(2)}) collective-permute-start(bf16[128,256]{1,0:T(8,128)(2,1)S(1)} %slice_bitcast_fusion.19), channel_id=1, source_target_pairs={{0,2},{2,0},{1,3},{3,1},{4,6},{6,4},{5,7},{7,5},{8,10},{10,8},{9,1... | collective-permute-start | bytes 196616 | tf_op jit(solution)/shard_map/ppermute | solution.py:16
  (19 other events, 147.0 us)
Sparse Core Ops, SparseCore 0:
  11.6 39.5 all-gather.2
  53.0 39.1 all-gather.4
  118.1 103.4 reduce-scatter.1
where the time goes:
time: 262 us; the launch traced here: 261 us
  waiting for transfers between devices  86.3 us (33%)
  starting transfers between devices  77.1 us (29%)
  Pallas kernels  28.2 us (11%)
  local copies, waits for them, and re-layouts  21.6 us (8%)
  matrix products  19.8 us (8%)
  between operations  14.1 us (5%)
  other arithmetic  14 us (5%)
    ppermute x27, starting transfers between devices, shift(): lax.ppermute(value, axis, [(i, (i + by) % size) for i in range(size)])  61.4 us
    ppermute x27, waiting for transfers between devices, shift(): lax.ppermute(value, axis, [(i, (i + by) % size) for i in range(size)])  51.8 us
    all_to_all x3, waiting for transfers between devices, swap(): return lax.all_to_all(value, axes, 0, 0, tiled=True)  34.5 us
    all_to_all x3, starting transfers between devices, swap(): return lax.all_to_all(value, axes, 0, 0, tiled=True)  15.4 us
    pallas_call x1, Pallas kernels, down_product(): pl.pallas_call(kernel, grid_spec=pltpu.PrefetchScalarGridSpec(num_scalar_...  11.7 us
    pallas_call x1, Pallas kernels, act_product(): pl.pallas_call(kernel, grid_spec=pltpu.PrefetchScalarGridSpec(num_scalar_...  9.63 us
    sub x1, matrix products, on_device(): weights = jnp.exp(scores - highest)  6.22 us
    unnamed x25, local copies, waits for them, and re-layouts  5.35 us
  transfers between devices with their start and end apart: 33, of which 14 were waited for; matrix products, arithmetic and copies ran while one was open for 18% of the time, Pallas kernels for 6%

commit v1 on v0

--- a/solution.py
+++ b/solution.py
@@ -288,13 +288,14 @@
     other_proj = shift(out_proj, "zh", 1)
     spots, flat, other_proj = meet(spots, flat, other_proj)
     act_all = swap(act_in, GROUP)
+    cols_in, act_all = meet(cols_in, act_all)
+    cols_all = swap(cols_in, CHIPS)
 
     where = jnp.stack([y, core, zh, lax.axis_index("x")]).astype(jnp.int32)
     down = down_product(spots, pieces, act_all)
 
-    cols_in, spots, where, down = meet(cols_in, spots, where, down)
+    spots, where, down = meet(spots, where, down)
     down_grad = lax.psum_scatter(down, SEQUENCES, scatter_dimension=0, tiled=True).astype(F32)
-    cols_all = swap(cols_in, CHIPS)
 
     part = act_product(spots, pieces, w_down)
 

time: 262 us -> 262 us (level)
  no operation moved by 1% of the time
where the time goes in v1:
time: 262 us; the launch traced here: 261 us
  waiting for transfers between devices  86.3 us (33%)
  starting transfers between devices  77.1 us (29%)
  Pallas kernels  28.2 us (11%)
  local copies, waits for them, and re-layouts  21.6 us (8%)
  matrix products  19.8 us (8%)
  between operations  14.1 us (5%)
  other arithmetic  14 us (5%)
    ppermute x27, starting transfers between devices, shift(): lax.ppermute(value, axis, [(i, (i + by) % size) for i in range(size)])  61.4 us
    ppermute x27, waiting for transfers between devices, shift(): lax.ppermute(value, axis, [(i, (i + by) % size) for i in range(size)])  51.8 us
    all_to_all x3, waiting for transfers between devices, swap(): return lax.all_to_all(value, axes, 0, 0, tiled=True)  34.5 us
    all_to_all x3, starting transfers between devices, swap(): return lax.all_to_all(value, axes, 0, 0, tiled=True)  15.4 us
    pallas_call x1, Pallas kernels, down_product(): pl.pallas_call(kernel, grid_spec=pltpu.PrefetchScalarGridSpec(num_scalar_...  11.7 us
    pallas_call x1, Pallas kernels, act_product(): pl.pallas_call(kernel, grid_spec=pltpu.PrefetchScalarGridSpec(num_scalar_...  9.63 us
    sub x1, matrix products, on_device(): weights = jnp.exp(scores - highest)  6.22 us
    unnamed x25, local copies, waits for them, and re-layouts  5.35 us
  transfers between devices with their start and end apart: 33, of which 14 were waited for; matrix products, arithmetic and copies ran while one was open for 18% of the time, Pallas kernels for 6%

profile of v1, /device:TPU:6, one launch (start us, length us, event | category | flops | bytes accessed | tf_op | source)
XLA Modules:
  0.0 261.2 jit_solution(18111138442802704051)
XLA Ops:
  13.0 7.3 %collective-permute-start = (bf16[128,256]{1,0:T(8,128)(2,1)S(1)}, bf16[128,256]{1,0:T(8,128)(2,1)S(1)}, u32[]{:S(2)}, u32[]{:S(2)}) collective-permute-start(bf16[128,256]{1,0:T(8,128)(2,1)S(1)} %constant_dynamic-update-slice_fusion), channel_id=1, source_target_pairs={{0,2},{2,0},{1,3},{3,1},{4,6},{6,4},{5,7},{7,5},{8,10},{10,8},{9,1... | collective-permute-start | bytes 196616 | tf_op jit(solution)/shard_map/ppermute | solution.py:16
  22.7 6.4 %collective-permute-start.5 = (bf16[40,6144]{1,0:T(8,128)(2,1)}, bf16[40,6144]{1,0:T(8,128)(2,1)}, u32[]{:S(2)}, u32[]{:S(2)}) collective-permute-start(bf16[40,6144]{1,0:T(8,128)(2,1)} %fusion.1), channel_id=1, source_target_pairs={{0,2},{2,0},{1,3},{3,1},{4,6},{6,4},{5,7},{7,5},{8,10},{10,8},{9,1... | collective-permute-start | bytes 1474568 | tf_op jit(solution)/shard_map/ppermute | solution.py:16
  35.5 5.9 %collective-permute-done.5 = bf16[40,6144]{1,0:T(8,128)(2,1)} collective-permute-done((bf16[40,6144]{1,0:T(8,128)(2,1)}, bf16[40,6144]{1,0:T(8,128)(2,1)}, u32[]{:S(2)}, u32[]{:S(2)}) %collective-permute-start.5) | collective-permute-done | bytes 491552 | tf_op jit(solution)/shard_map/ppermute | solution.py:16
  53.6 11.7 %collective-permute-start.6 = (bf16[768,384]{1,0:T(8,128)(2,1)S(1)}, bf16[768,384]{1,0:T(8,128)(2,1)S(1)}, u32[]{:S(2)}, u32[]{:S(2)}) collective-permute-start(bf16[768,384]{1,0:T(8,128)(2,1)S(1)} %copy-done), channel_id=1, source_target_pairs={{0,2},{2,0},{1,3},{3,1},{4,6},{6,4},{5,7},{7,5},{8,10},{10,8},{9,1... | collective-permute-start | bytes 1769480 | tf_op jit(solution)/shard_map/ppermute | solution.py:16
  65.4 3.9 %all-to-all-start = ((bf16[16,40,512]{2,1,0:T(8,128)(2,1)}), bf16[16,40,512]{2,1,0:T(8,128)(2,1)S(1)}, u32[]{:S(2)}, u32[]{:S(2)}) async-start(bf16[16,40,512]{2,1,0:T(8,128)(2,1)} %bitcast.154), calls=%async_computation | async-start | bytes 1310720 | tf_op jit(solution)/shard_map/all_to_all | solution.py:32
  71.5 6.2 %fusion.43 = (f32[6,128]{1,0:T(8,128)S(1)}, f32[6,128,2048]{1,2,0:T(8,128)}) fusion(pred[128,2048]{0,1:T(8,128)(4,1)} %broadcast_compare_fusion, bf16[128,6,128]{0,2,1:T(8,128)(2,1)} %bitcast.176, bf16[2048,256]{1,0:T(8,128)(2,1)S(1)} %bitcast.158), kind=kOutput, calls=%fused_computation.106 | convolution fusion | flops 408946688 | bytes 7277568 | tf_op jit(solution)/shard_map/sub | solution.py:282
  77.7 3.4 %fusion.8 = bf16[6,128,2048]{1,2,0:T(8,128)(2,1)S(1)} fusion(f32[6,128,2048]{1,2,0:T(8,128)} %get-tuple-element.96, f32[6,128]{1,0:T(8,128)S(1)} %get-tuple-element.95), kind=kLoop, calls=%fused_computation.13 | loop fusion | flops 3145728 | bytes 9440256 | tf_op jit(solution)/shard_map/convert_element_type | solution.py:284
  82.9 22.5 %all-to-all-done.act_ref = bf16[16,40,512]{2,1,0:T(8,128)(2,1)S(1)} async-done(((bf16[16,40,512]{2,1,0:T(8,128)(2,1)}), bf16[16,40,512]{2,1,0:T(8,128)(2,1)S(1)}, u32[]{:S(2)}, u32[]{:S(2)}) %all-to-all-start) | async-done | bytes 655392 | tf_op jit(solution)/shard_map/all_to_all | solution.py:32
  106.3 11.7 %shard_map.136 = bf16[6144,512]{1,0:T(8,128)(2,1)} custom-call(s32[16]{0:T(128)} %stack.130.spots_ref, bf16[320,6144]{1,0:T(8,128)(2,1)} %all-gather.3.cloned.1.call-done.near_ref.refs_0_, bf16[320,6144]{1,0:T(8,128)(2,1)} %all-gather.5.cloned.1.call-done.far_ref.refs_1_, bf16[16,40,512]{2,1,0:T(8,128)(2,1)} %copy-done.6), custom_call_target="tpu_custom_call" | custom-call | flops 4026531840 | bytes 16777216 | tf_op jit(solution)/shard_map/pallas_call | solution.py:71
  118.0 3.9 %all-to-all-start.2 = ((bf16[8,128,768]{2,1,0:T(8,128)(2,1)}), bf16[8,128,768]{2,1,0:T(8,128)(2,1)S(1)}, u32[]{:S(2)}, u32[]{:S(2)}) async-start(bf16[8,128,768]{2,1,0:T(8,128)(2,1)} %reshape.168), calls=%async_computation.2 | async-start | bytes 3145728 | tf_op jit(solution)/shard_map/all_to_all | solution.py:32
  121.9 9.6 %shard_map.137 = bf16[16,40,512]{2,1,0:T(8,128)(2,1)} custom-call(s32[16]{0:T(128)} %stack.130.spots_ref, bf16[320,6144]{1,0:T(8,128)(2,1)} %all-gather.3.cloned.1.call-done.near_ref.refs_0_, bf16[320,6144]{1,0:T(8,128)(2,1)} %all-gather.5.cloned.1.call-done.far_ref.refs_1_, bf16[6144,512]{1,0:T(8,128)(2,1)} %refs_2_.1), custom_call_target="tpu_custom_call" | custom-call | flops 4026531840 | bytes 16777216 | tf_op jit(solution)/shard_map/pallas_call | solution.py:115
  131.5 12.0 %all-to-all-done.2.refs_0_.refs_1_.refs_2_.refs_3_.cols_ref = bf16[8,128,768]{2,1,0:T(8,128)(2,1)S(1)} async-done(((bf16[8,128,768]{2,1,0:T(8,128)(2,1)}), bf16[8,128,768]{2,1,0:T(8,128)(2,1)S(1)}, u32[]{:S(2)}, u32[]{:S(2)}) %all-to-all-start.2) | async-done | bytes 1572896 | tf_op jit(solution)/shard_map/all_to_all | solution.py:32
  143.4 3.6 %shard_map.138 = (bf16[4,128,768]{2,1,0:T(8,128)(2,1)S(1)}, bf16[4,128,768]{2,1,0:T(8,128)(2,1)}) custom-call(s32[4]{0:T(128)S(1)} %pad_add_fusion.where_ref, bf16[8,128,768]{2,1,0:T(8,128)(2,1)S(1)} %all-to-all-done.2.refs_0_.refs_1_.refs_2_.refs_3_.cols_ref, bf16[8,128,768]{2,1,0:T(8,128)(2,1)S(1)} %all-to-all-done.2.refs_0_.refs_1_.refs_2_.refs_3_.cols_ref, ...), custom_call_target="tpu_custom_call" | custom-call | flops 1207959552 | bytes 6291456 | tf_op jit(solution)/shard_map/pallas_call | solution.py:167
  155.3 9.9 %collective-permute-done.13 = bf16[128,768]{1,0:T(8,128)(2,1)S(1)} collective-permute-done((bf16[128,768]{1,0:T(8,128)(2,1)S(1)}, bf16[128,768]{1,0:T(8,128)(2,1)S(1)}, u32[]{:S(2)}, u32[]{:S(2)}) %collective-permute-start.13) | collective-permute-done | bytes 196640 | tf_op jit(solution)/shard_map/ppermute | solution.py:16
  166.5 6.3 %collective-permute-done.8 = bf16[128,768]{1,0:T(8,128)(2,1)S(1)} collective-permute-done((bf16[128,768]{1,0:T(8,128)(2,1)S(1)}, bf16[128,768]{1,0:T(8,128)(2,1)S(1)}, u32[]{:S(2)}, u32[]{:S(2)}) %collective-permute-start.8) | collective-permute-done | bytes 196640 | tf_op jit(solution)/shard_map/ppermute | solution.py:16
  175.7 4.2 %fusion.3 = bf16[6,128,2048]{1,2,0:T(8,128)(2,1)S(1)} fusion(bf16[128,6,128]{0,2,1:T(8,128)(2,1)S(1)} %bitcast.165, f32[6,128]{1,0:T(8,128)S(1)} %bitcast.183, f32[6,128,2048]{1,2,0:T(8,128)} %get-tuple-element.96, f32[6,128]{1,0:T(8,128)S(1)} %get-tuple-element.95, bf16[2048,256]{1,0:T(8,128)(2,1)} %bitcast.160), kind=kOutput, calls=%fused_computation.5 | convolution fusion | flops 408944640 | bytes 10164224 | tf_op jit(solution)/shard_map/qhd,kd->hqk/dot_general | solution.py:314
  185.6 7.7 %all-to-all-start.1 = ((bf16[16,40,512]{2,1,0:T(8,128)(2,1)}), bf16[16,40,512]{2,1,0:T(8,128)(2,1)}, u32[]{:S(2)}, u32[]{:S(2)}) async-start(bf16[16,40,512]{2,1,0:T(8,128)(2,1)} %shard_map.137), calls=%async_computation.1 | async-start | bytes 1310720 | tf_op jit(solution)/shard_map/all_to_all | solution.py:32
  193.2 3.2 %shard_map.139 = (bf16[4,48,768]{2,1,0:T(8,128)(2,1)S(1)}, bf16[4,48,768]{2,1,0:T(8,128)(2,1)}, bf16[4,48,768]{2,1,0:T(8,128)(2,1)}, bf16[4,48,768]{2,1,0:T(8,128)(2,1)}) custom-call(s32[4]{0:T(128)S(1)} %pad_add_fusion.where_ref, bf16[4,128,768]{2,1,0:T(8,128)(2,1)S(1)} %pad_maximum_fusion.1.mine_ref, ...), custom_call_target="tpu_custom_call" | custom-call | flops 1207959552 | bytes 6291456 | tf_op jit(solution)/shard_map/pallas_call | solution.py:209
  206.8 3.2 %collective-permute-start.21 = (bf16[2,128,256]{2,1,0:T(8,128)(2,1)S(1)}, bf16[2,128,256]{2,1,0:T(8,128)(2,1)S(1)}, u32[]{:S(2)}, u32[]{:S(2)}) collective-permute-start(bf16[2,128,256]{2,1,0:T(8,128)(2,1)S(1)} %get-tuple-element.84), channel_id=1, source_target_pairs={{0,12},{4,0},{8,4},{12,8},{1,13},{5,1},{9,5},{13,9},{2,14},{6,2},{... | collective-permute-start | bytes 393224 | tf_op jit(solution)/shard_map/ppermute | solution.py:16
  212.0 8.9 %collective-permute-done.16 = bf16[4,48,768]{2,1,0:T(8,128)(2,1)S(1)} collective-permute-done((bf16[4,48,768]{2,1,0:T(8,128)(2,1)}, bf16[4,48,768]{2,1,0:T(8,128)(2,1)S(1)}, u32[]{:S(2)}, u32[]{:S(2)}) %collective-permute-start.16) | collective-permute-done | bytes 294944 | tf_op jit(solution)/shard_map/ppermute | solution.py:16
  225.7 4.2 %collective-permute-start.22 = (bf16[128,256]{1,0:T(8,128)(2,1)S(1)}, bf16[128,256]{1,0:T(8,128)(2,1)S(1)}, u32[]{:S(2)}, u32[]{:S(2)}) collective-permute-start(bf16[128,256]{1,0:T(8,128)(2,1)S(1)} %slice_bitcast_fusion.19), channel_id=1, source_target_pairs={{0,2},{2,0},{1,3},{3,1},{4,6},{6,4},{5,7},{7,5},{8,10},{10,8},{9,1... | collective-permute-start | bytes 196616 | tf_op jit(solution)/shard_map/ppermute | solution.py:16
  229.9 6.5 %collective-permute-start.25 = (bf16[48,768]{1,0:T(8,128)(2,1)S(1)}, bf16[48,768]{1,0:T(8,128)(2,1)S(1)}, u32[]{:S(2)}, u32[]{:S(2)}) collective-permute-start(bf16[48,768]{1,0:T(8,128)(2,1)S(1)} %get-tuple-element.89), channel_id=1, source_target_pairs={{0,192},{64,0},{128,64},{192,128},{1,193},{65,1},{129,65},{193,129... | collective-permute-start | bytes 221192 | tf_op jit(solution)/shard_map/ppermute | solution.py:16
  239.0 5.0 %collective-permute-done.24 = bf16[48,768]{1,0:T(8,128)(2,1)S(1)} collective-permute-done((bf16[48,768]{1,0:T(8,128)(2,1)S(1)}, bf16[48,768]{1,0:T(8,128)(2,1)S(1)}, u32[]{:S(2)}, u32[]{:S(2)}) %collective-permute-start.24) | collective-permute-done | bytes 73760 | tf_op jit(solution)/shard_map/ppermute | solution.py:16
  246.6 5.4 %collective-permute-done.26 = bf16[48,384]{1,0:T(8,128)(2,1)S(1)} collective-permute-done((bf16[48,384]{1,0:T(8,128)(2,1)S(1)}, bf16[48,384]{1,0:T(8,128)(2,1)S(1)}, u32[]{:S(2)}, u32[]{:S(2)}) %collective-permute-start.26) | collective-permute-done | bytes 36896 | tf_op jit(solution)/shard_map/ppermute | solution.py:16
  (122 shorter events, 74.5 us)
Async XLA Ops:
  7.2 98.3 %all-gather.3.cloned.1.call-start = ((), (), s32[]{:S(2)}) async-start(), calls=%async_computation.4 | async-start | bytes 4423680 | tf_op jit(solution)/shard_map/all_gather | solution.py:253
  11.4 94.0 %all-gather.5.cloned.1.call-start = ((), (), s32[]{:S(2)}) async-start(), calls=%async_computation.5 | async-start | bytes 4423680 | tf_op jit(solution)/shard_map/all_gather | solution.py:261
  13.0 9.7 %collective-permute-start = (bf16[128,256]{1,0:T(8,128)(2,1)S(1)}, bf16[128,256]{1,0:T(8,128)(2,1)S(1)}, u32[]{:S(2)}, u32[]{:S(2)}) collective-permute-start(bf16[128,256]{1,0:T(8,128)(2,1)S(1)} %constant_dynamic-update-slice_fusion), channel_id=1, source_target_pairs={{0,2},{2,0},{1,3},{3,1},{4,6},{6,4},{5,7},{7,5},{8,10},{10,8},{9,1... | collective-permute-start | bytes 196616 | tf_op jit(solution)/shard_map/ppermute | solution.py:16
  22.7 18.7 %collective-permute-start.5 = (bf16[40,6144]{1,0:T(8,128)(2,1)}, bf16[40,6144]{1,0:T(8,128)(2,1)}, u32[]{:S(2)}, u32[]{:S(2)}) collective-permute-start(bf16[40,6144]{1,0:T(8,128)(2,1)} %fusion.1), channel_id=1, source_target_pairs={{0,2},{2,0},{1,3},{3,1},{4,6},{6,4},{5,7},{7,5},{8,10},{10,8},{9,1... | collective-permute-start | bytes 1474568 | tf_op jit(solution)/shard_map/ppermute | solution.py:16
  52.4 17.1 %collective-permute-start.4 = (bf16[4,2,128,256]{3,2,1,0:T(8,128)(2,1)S(1)}, bf16[4,2,128,256]{3,2,1,0:T(8,128)(2,1)S(1)}, u32[]{:S(2)}, u32[]{:S(2)}) collective-permute-start(bf16[4,2,128,256]{3,2,1,0:T(8,128)(2,1)S(1)} %get-tuple-element.87), channel_id=1, source_target_pairs={{0,1},{1,0},{2,3},{3,2},{4,5},{5,4},{6,7},{7,6},{8,9},{9,8},{10,11... | collective-permute-start | bytes 1572872 | tf_op jit(solution)/shard_map/ppermute | solution.py:16
  53.6 29.2 %collective-permute-start.6 = (bf16[768,384]{1,0:T(8,128)(2,1)S(1)}, bf16[768,384]{1,0:T(8,128)(2,1)S(1)}, u32[]{:S(2)}, u32[]{:S(2)}) collective-permute-start(bf16[768,384]{1,0:T(8,128)(2,1)S(1)} %copy-done), channel_id=1, source_target_pairs={{0,2},{2,0},{1,3},{3,1},{4,6},{6,4},{5,7},{7,5},{8,10},{10,8},{9,1... | collective-permute-start | bytes 1769480 | tf_op jit(solution)/shard_map/ppermute | solution.py:16
  65.4 40.1 %all-to-all-start = ((bf16[16,40,512]{2,1,0:T(8,128)(2,1)}), bf16[16,40,512]{2,1,0:T(8,128)(2,1)S(1)}, u32[]{:S(2)}, u32[]{:S(2)}) async-start(bf16[16,40,512]{2,1,0:T(8,128)(2,1)} %bitcast.154), calls=%async_computation | async-start | bytes 1310720 | tf_op jit(solution)/shard_map/all_to_all | solution.py:32
  69.3 183.4 %reduce-scatter.2.cloned.1.call-start = ((), (), s32[]{:S(2)}) async-start(), calls=%async_computation.6 | async-start | bytes 6684672 | tf_op jit(solution)/shard_map/reduce_scatter | solution.py:298
  118.0 25.4 %all-to-all-start.2 = ((bf16[8,128,768]{2,1,0:T(8,128)(2,1)}), bf16[8,128,768]{2,1,0:T(8,128)(2,1)S(1)}, u32[]{:S(2)}, u32[]{:S(2)}) async-start(bf16[8,128,768]{2,1,0:T(8,128)(2,1)} %reshape.168), calls=%async_computation.2 | async-start | bytes 3145728 | tf_op jit(solution)/shard_map/all_to_all | solution.py:32
  148.2 17.0 %collective-permute-start.13 = (bf16[128,768]{1,0:T(8,128)(2,1)S(1)}, bf16[128,768]{1,0:T(8,128)(2,1)S(1)}, u32[]{:S(2)}, u32[]{:S(2)}) collective-permute-start(bf16[128,768]{1,0:T(8,128)(2,1)S(1)} %copy.57), channel_id=1, source_target_pairs={{0,4},{4,8},{8,12},{12,0},{1,5},{5,9},{9,13},{13,1},{2,6},{6,10},{... | collective-permute-start | bytes 589832 | tf_op jit(solution)/shard_map/ppermute | solution.py:16
  148.8 16.4 %collective-permute-start.12 = (bf16[128,768]{1,0:T(8,128)(2,1)S(1)}, bf16[128,768]{1,0:T(8,128)(2,1)S(1)}, u32[]{:S(2)}, u32[]{:S(2)}) collective-permute-start(bf16[128,768]{1,0:T(8,128)(2,1)S(1)} %copy.57), channel_id=1, source_target_pairs={{0,8},{4,12},{8,0},{12,4},{1,9},{5,13},{9,1},{13,5},{2,10},{6,14},... | collective-permute-start | bytes 589832 | tf_op jit(solution)/shard_map/ppermute | solution.py:16
  150.9 14.3 %collective-permute-start.11 = (bf16[128,768]{1,0:T(8,128)(2,1)S(1)}, bf16[128,768]{1,0:T(8,128)(2,1)S(1)}, u32[]{:S(2)}, u32[]{:S(2)}) collective-permute-start(bf16[128,768]{1,0:T(8,128)(2,1)S(1)} %copy.57), channel_id=1, source_target_pairs={{0,12},{4,0},{8,4},{12,8},{1,13},{5,1},{9,5},{13,9},{2,14},{6,2},{... | collective-permute-start | bytes 589832 | tf_op jit(solution)/shard_map/ppermute | solution.py:16
  151.8 14.7 %collective-permute-start.10 = (bf16[128,768]{1,0:T(8,128)(2,1)S(1)}, bf16[128,768]{1,0:T(8,128)(2,1)S(1)}, u32[]{:S(2)}, u32[]{:S(2)}) collective-permute-start(bf16[128,768]{1,0:T(8,128)(2,1)S(1)} %get-tuple-element.81), channel_id=1, source_target_pairs={{0,12},{4,0},{8,4},{12,8},{1,13},{5,1},{9,5},{13,9},{2,14},{6,2},{... | collective-permute-start | bytes 589832 | tf_op jit(solution)/shard_map/ppermute | solution.py:16
  153.2 13.3 %collective-permute-start.9 = (bf16[128,768]{1,0:T(8,128)(2,1)S(1)}, bf16[128,768]{1,0:T(8,128)(2,1)S(1)}, u32[]{:S(2)}, u32[]{:S(2)}) collective-permute-start(bf16[128,768]{1,0:T(8,128)(2,1)S(1)} %get-tuple-element.82), channel_id=1, source_target_pairs={{0,8},{4,12},{8,0},{12,4},{1,9},{5,13},{9,1},{13,5},{2,10},{6,14},... | collective-permute-start | bytes 589832 | tf_op jit(solution)/shard_map/ppermute | solution.py:16
  165.3 27.9 %collective-permute-start.14 = (bf16[4,128,768]{2,1,0:T(8,128)(2,1)S(1)}, bf16[4,128,768]{2,1,0:T(8,128)(2,1)S(1)}, u32[]{:S(2)}, u32[]{:S(2)}) collective-permute-start(bf16[4,128,768]{2,1,0:T(8,128)(2,1)S(1)} %pad_maximum_fusion.1.mine_ref), channel_id=1, source_target_pairs={{0,1},{1,0},{2,3},{3,2},{4,5},{5,4},{6,7},{7,6},{8,9},{9,8},{10,11... | collective-permute-start | bytes 2359304 | tf_op jit(solution)/shard_map/ppermute | solution.py:16
  185.6 20.0 %collective-permute-start.18 = (bf16[4,2,128,256]{3,2,1,0:T(8,128)(2,1)}, bf16[4,2,128,256]{3,2,1,0:T(8,128)(2,1)}, u32[]{:S(2)}, u32[]{:S(2)}) collective-permute-start(bf16[4,2,128,256]{3,2,1,0:T(8,128)(2,1)} %bitcast.171), channel_id=1, source_target_pairs={{0,1},{1,0},{2,3},{3,2},{4,5},{5,4},{6,7},{7,6},{8,9},{9,8},{10,11... | collective-permute-start | bytes 1572872 | tf_op jit(solution)/shard_map/ppermute | solution.py:16
  185.6 37.5 %all-to-all-start.1 = ((bf16[16,40,512]{2,1,0:T(8,128)(2,1)}), bf16[16,40,512]{2,1,0:T(8,128)(2,1)}, u32[]{:S(2)}, u32[]{:S(2)}) async-start(bf16[16,40,512]{2,1,0:T(8,128)(2,1)} %shard_map.137), calls=%async_computation.1 | async-start | bytes 1310720 | tf_op jit(solution)/shard_map/all_to_all | solution.py:32
  196.4 14.4 %collective-permute-start.17 = (bf16[4,48,768]{2,1,0:T(8,128)(2,1)}, bf16[4,48,768]{2,1,0:T(8,128)(2,1)S(1)}, u32[]{:S(2)}, u32[]{:S(2)}) collective-permute-start(bf16[4,48,768]{2,1,0:T(8,128)(2,1)} %get-tuple-element.54), channel_id=1, source_target_pairs={{0,48},{16,0},{32,16},{48,32},{1,49},{17,1},{33,17},{49,33},{2,50}... | collective-permute-start | bytes 884744 | tf_op jit(solution)/shard_map/ppermute | solution.py:16
  197.3 23.6 %collective-permute-start.16 = (bf16[4,48,768]{2,1,0:T(8,128)(2,1)}, bf16[4,48,768]{2,1,0:T(8,128)(2,1)S(1)}, u32[]{:S(2)}, u32[]{:S(2)}) collective-permute-start(bf16[4,48,768]{2,1,0:T(8,128)(2,1)} %get-tuple-element.53), channel_id=1, source_target_pairs={{0,32},{16,48},{32,0},{48,16},{1,33},{17,49},{33,1},{49,17},{2,34}... | collective-permute-start | bytes 884744 | tf_op jit(solution)/shard_map/ppermute | solution.py:16
  198.5 24.4 %collective-permute-start.15 = (bf16[4,48,768]{2,1,0:T(8,128)(2,1)}, bf16[4,48,768]{2,1,0:T(8,128)(2,1)S(1)}, u32[]{:S(2)}, u32[]{:S(2)}) collective-permute-start(bf16[4,48,768]{2,1,0:T(8,128)(2,1)} %get-tuple-element.52), channel_id=1, source_target_pairs={{0,16},{16,32},{32,48},{48,0},{1,17},{17,33},{33,49},{49,1},{2,18}... | collective-permute-start | bytes 884744 | tf_op jit(solution)/shard_map/ppermute | solution.py:16
  206.8 16.2 %collective-permute-start.21 = (bf16[2,128,256]{2,1,0:T(8,128)(2,1)S(1)}, bf16[2,128,256]{2,1,0:T(8,128)(2,1)S(1)}, u32[]{:S(2)}, u32[]{:S(2)}) collective-permute-start(bf16[2,128,256]{2,1,0:T(8,128)(2,1)S(1)} %get-tuple-element.84), channel_id=1, source_target_pairs={{0,12},{4,0},{8,4},{12,8},{1,13},{5,1},{9,5},{13,9},{2,14},{6,2},{... | collective-permute-start | bytes 393224 | tf_op jit(solution)/shard_map/ppermute | solution.py:16
  210.0 13.1 %collective-permute-start.20 = (bf16[2,128,256]{2,1,0:T(8,128)(2,1)S(1)}, bf16[2,128,256]{2,1,0:T(8,128)(2,1)S(1)}, u32[]{:S(2)}, u32[]{:S(2)}) collective-permute-start(bf16[2,128,256]{2,1,0:T(8,128)(2,1)S(1)} %get-tuple-element.85), channel_id=1, source_target_pairs={{0,8},{4,12},{8,0},{12,4},{1,9},{5,13},{9,1},{13,5},{2,10},{6,14},... | collective-permute-start | bytes 393224 | tf_op jit(solution)/shard_map/ppermute | solution.py:16
  210.8 12.2 %collective-permute-start.19 = (bf16[2,128,256]{2,1,0:T(8,128)(2,1)S(1)}, bf16[2,128,256]{2,1,0:T(8,128)(2,1)S(1)}, u32[]{:S(2)}, u32[]{:S(2)}) collective-permute-start(bf16[2,128,256]{2,1,0:T(8,128)(2,1)S(1)} %get-tuple-element.83), channel_id=1, source_target_pairs={{0,4},{4,8},{8,12},{12,0},{1,5},{5,9},{9,13},{13,1},{2,6},{6,10},{... | collective-permute-start | bytes 393224 | tf_op jit(solution)/shard_map/ppermute | solution.py:16
  225.7 11.7 %collective-permute-start.22 = (bf16[128,256]{1,0:T(8,128)(2,1)S(1)}, bf16[128,256]{1,0:T(8,128)(2,1)S(1)}, u32[]{:S(2)}, u32[]{:S(2)}) collective-permute-start(bf16[128,256]{1,0:T(8,128)(2,1)S(1)} %slice_bitcast_fusion.19), channel_id=1, source_target_pairs={{0,2},{2,0},{1,3},{3,1},{4,6},{6,4},{5,7},{7,5},{8,10},{10,8},{9,1... | collective-permute-start | bytes 196616 | tf_op jit(solution)/shard_map/ppermute | solution.py:16
  (19 other events, 147.0 us)
Sparse Core Ops, SparseCore 0:
  11.6 39.5 all-gather.2
  53.0 39.1 all-gather.4
  118.1 103.4 reduce-scatter.1
